TPU v7x, 32 devices: a whole 2x2x4 slice. The times are simulated.
32 devices in a mesh: groups: 1, db: 16 (over z, y, core), seq: 2 (over x), mp: 1.
Axes of the slice: x: 2, y: 2, z: 4, core: 2. Of those that a mesh axis runs over, the one named last changes fastest.
Arguments:
- queries: bfloat16 [16, 896, 2048], P(('groups', 'db'), 'seq', 'mp'), may hold values from -110 to 110
- database: bfloat16 [64, 128, 896], P(('groups', 'db')), may hold values from -6 to 6
- nb_owner: int32 [16, 28], P(('groups', 'db'), 'seq'), may hold values from 0 to 15, as said below
- nb_row: int32 [16, 28], P(('groups', 'db'), 'seq'), may hold values from 0 to 3
- kv_weight: bfloat16 [896, 2, 2048], P('seq', None, 'mp'), may hold values from -0.1875 to 0.1875
Outputs:
- attended: bfloat16 [16, 896, 2048], P(('groups', 'db'), 'seq', 'mp')
Inputs may be any that keep to these rules, and one draw needn't show every extreme that they name: `nb_owner`: within each device's aligned block of 14 consecutive slots of a sequence, no shard is named more than 2 times; one shard, the same for every block, is named exactly 2 times in every block.
All inputs are finite; a program needn't handle non-finite values.
Results may differ from a plain program's by a relative error of at most 0.015.
The roundings to bfloat16 on the way count: a program that leaves them out, or rounds other values in their place, can miss the bound.
Values may be sent and summed in bfloat16 or wider, within the bound.
A program may use at most 128 MiB of HBM per device.

v0:
```python
import jax
import jax.numpy as jnp
from jax import lax
from jax.sharding import PartitionSpec as P

HD = 128
KNN = 2


def passed_along(x, axis, by):
    devices = lax.axis_size(axis)
    pairs = [(i, i + by) for i in range(devices) if 0 <= i + by < devices]
    return lax.ppermute(x, axis, pairs)


def per_device(queries, database, nb_owner, nb_row, kv_weight):
    n_db = lax.axis_size("db")
    owners = nb_owner[0]
    wanted = nb_row[0]
    slots = owners.shape[0]
    cap = max(2, (2 * slots + n_db - 1) // n_db)
    order = jnp.arange(slots, dtype=jnp.int32)
    before = (owners[:, None] == owners[None, :]) & (order[None, :] < order[:, None])
    rank = jnp.sum(before.astype(jnp.int32), axis=1)
    place = owners * cap + rank
    cells = jnp.arange(n_db * cap, dtype=jnp.int32)
    match = place[None, :] == cells[:, None]
    request = jnp.sum(jnp.where(match, wanted[None, :] + 1, 0), axis=1) - 1
    incoming = lax.all_to_all(
        request.reshape(n_db, cap), "db", split_axis=0, concat_axis=0, tiled=True
    )
    lookup = jnp.maximum(incoming, 0).reshape(-1)
    n_mp = lax.axis_size("mp")
    which = lax.axis_index("mp")
    length = database.shape[1] // n_mp
    local_part = lax.dynamic_slice_in_dim(database, which * length, length, 1)
    picked = jnp.take(local_part, lookup, axis=0).reshape(n_db, cap, length, database.shape[2])
    returned = lax.all_to_all(picked, "db", split_axis=0, concat_axis=0, tiled=True)
    mine = jnp.take(returned.reshape(n_db * cap, length, database.shape[2]), place, axis=0)
    fetched = lax.all_gather(mine, "mp", axis=1, tiled=True)
    rows = fetched.reshape(-1, fetched.shape[2])
    span = KNN * fetched.shape[1]
    stretches = slots // KNN
    head_cols = kv_weight.shape[2]
    full_weight = lax.all_gather(kv_weight, "seq", axis=0, tiled=True)
    projected = jnp.dot(
        rows, full_weight.reshape(full_weight.shape[0], -1), preferred_element_type=jnp.float32
    ).astype(jnp.bfloat16)
    blocks = projected.reshape(-1, span, 2, head_cols)
    earlier = passed_along(blocks[-1], "seq", 1)
    keyvals = jnp.concatenate([earlier[None], blocks[:-1]], axis=0)
    heads = head_cols // HD
    query = queries[0].reshape(stretches, -1, heads, HD)
    keys = keyvals[:, :, 0].reshape(stretches, span, heads, HD)
    values = keyvals[:, :, 1].reshape(stretches, span, heads, HD)
    scores = jnp.einsum(
        "cqhd,ckhd->chqk", query, keys, preferred_element_type=jnp.float32
    ) * HD ** (-0.5)
    top = jnp.max(scores, axis=-1, keepdims=True)
    weights = jnp.exp(scores - top)
    probs = (weights / jnp.sum(weights, axis=-1, keepdims=True)).astype(jnp.bfloat16)
    mixed = jnp.einsum("chqk,ckhd->cqhd", probs, values, preferred_element_type=jnp.float32)
    return mixed.astype(jnp.bfloat16).reshape(1, -1, head_cols)


def solution(mesh):
    return jax.shard_map(
        per_device,
        mesh=mesh,
        in_specs=(
            P(("groups", "db"), "seq", "mp"),
            P(("groups", "db"), None, None),
            P(("groups", "db"), "seq"),
            P(("groups", "db"), "seq"),
            P("seq", None, "mp"),
        ),
        out_specs=P(("groups", "db"), "seq", "mp"),
        check_vma=False,
    )
```

profile of v0, /device:TPU:16, one launch (start us, length us, event | category | flops | bytes accessed | tf_op | source)
XLA Modules:
  0.0 345.0 jit_solution(11298296368853842976)
XLA Ops:
  6.5 0.9 convert_reduce_fusion
  7.5 0.7 fusion.17
  8.2 0.1 select_reduce_fusion
  8.3 10.1 %all_to_all.11 = s32[16,1,2]{2,1,0:T(1,128)S(1)} all-to-all(s32[16,1,2]{2,1,0:T(1,128)S(1)} %bitcast.69), channel_id=1, replica_groups=mesh['groups'=1,'db'=16,'seq'=2,'mp'=1] {'db'}, dimensions={0} | all-to-all | bytes 256 | tf_op jit(solution)/shard_map/all_to_all | solution.py:29
  18.4 0.1 reshape.134
  18.5 0.1 copy.27
  18.7 0.1 copy.28
  18.8 4.4 %gather_fusion = bf16[32,128,896]{2,1,0:T(8,128)(2,1)} fusion(bf16[4,128,896]{2,1,0:T(8,128)(2,1)S(1)} %copy-done, s32[1024]{0:T(1024)S(1)} %pad_clamp_fusion.1), kind=kCustom, calls=%fused_computation | custom fusion | bytes 14680192 | tf_op jit(solution)/shard_map/jit(_take)/gather | solution.py:37
  23.1 6.9 %broadcast_select_fusion = bf16[16,2,128,896]{3,2,1,0:T(8,128)(2,1)} fusion(bf16[16,2,128,896]{3,2,1,0:T(8,128)(2,1)} %bitcast.61, pred[16,2]{1,0:T(8,128)(4,1)S(1)} %copy.28), kind=kLoop, calls=%fused_computation.13 | loop fusion | flops 3670016 | bytes 14680096 | tf_op jit(solution)/shard_map/jit(_take)/select_n | solution.py:37
  30.0 7.0 %all-to-all-start.1 = ((bf16[16,2,128,896]{3,2,1,0:T(8,128)(2,1)}), bf16[16,2,128,896]{3,2,1,0:T(8,128)(2,1)}, u32[]{:S(2)}, u32[]{:S(2)}) async-start(bf16[16,2,128,896]{3,2,1,0:T(8,128)(2,1)} %broadcast_select_fusion), calls=%async_computation.1 | async-start | bytes 14680064 | tf_op jit(solution)/shard_map/all_to_all | solution.py:38
  37.1 0.7 all-gather.2.cloned.1.call-update
  37.8 94.7 %all-gather.2.cloned.1.call-done = bf16[896,2,2048]{2,1,0:T(2,128)(2,1)} async-done(((bf16[448,2,2048]{2,1,0:T(2,128)(2,1)}), bf16[896,2,2048]{2,1,0:T(2,128)(2,1)}) %all-gather.2.cloned.1.call-update) | async-done | bytes 7340048 | tf_op jit(solution)/shard_map/all_gather | solution.py:45
  132.6 10.7 %copy.38 = bf16[112,8,2,2048]{3,1,2,0:T(8,128)(2,1)} copy(bf16[112,8,2,2048]{3,2,1,0:T(2,128)(2,1)} %bitcast.64) | data formatting | bytes 14680064
  143.3 53.8 %all-to-all-done.1 = bf16[16,2,128,896]{3,2,1,0:T(8,128)(2,1)} async-done(((bf16[16,2,128,896]{3,2,1,0:T(8,128)(2,1)}), bf16[16,2,128,896]{3,2,1,0:T(8,128)(2,1)}, u32[]{:S(2)}, u32[]{:S(2)}) %all-to-all-start.1) | async-done | bytes 7340064 | tf_op jit(solution)/shard_map/all_to_all | solution.py:38
  197.1 5.9 %gather_fusion.1 = bf16[14,128,896]{2,1,0:T(8,128)(2,1)} fusion(bf16[32,128,896]{2,1,0:T(8,128)(2,1)} %bitcast.7, s32[1024]{0:T(1024)S(1)} %pad_clamp_fusion), kind=kCustom, calls=%fused_computation.1 | custom fusion | bytes 6422584 | tf_op jit(solution)/shard_map/jit(_take)/gather | solution.py:39
  203.0 2.3 broadcast_select_fusion.1
  205.3 17.8 %convolution_convert_fusion = bf16[1792,4096]{1,0:T(8,128)(2,1)S(1)} fusion(bf16[1792,896]{1,0:T(8,128)(2,1)S(1)} %bitcast.66, bf16[896,4096]{1,0:T(8,128)(2,1)} %bitcast.65), kind=kOutput, calls=%fused_computation.3 | convolution fusion | flops 13160677376 | bytes 25231360 | tf_op jit(solution)/shard_map/dot_general | solution.py:46
  223.1 5.2 %copy-done.2 = bf16[1792,4096]{1,0:T(8,128)(2,1)} copy-done((bf16[1792,4096]{1,0:T(8,128)(2,1)}, bf16[1792,4096]{1,0:T(8,128)(2,1)S(1)}, u32[]{:S(2)}) %copy-start.2) | copy-done | bytes 14680088
  228.3 0.2 slice.25
  228.6 2.5 copy.37
  231.1 4.7 %collective-permute-start = (bf16[256,2,2048]{0,2,1:T(8,128)(2,1)}, bf16[256,2,2048]{0,2,1:T(8,128)(2,1)}, u32[]{:S(2)}, u32[]{:S(2)}) collective-permute-start(bf16[256,2,2048]{0,2,1:T(8,128)(2,1)} %bitcast.67), channel_id=1, source_target_pairs={{0,1},{2,3},{4,5},{6,7},{8,9},{10,11},{12,13},{14,15},{16,17},{18,... | collective-permute-start | bytes 6291464 | tf_op jit(solution)/shard_map/ppermute | solution.py:13
  235.8 2.0 copy.39
  237.8 10.9 %slice.26 = bf16[1536,4096]{1,0:T(8,128)(2,1)} slice(bf16[1792,4096]{1,0:T(8,128)(2,1)} %copy-done.2), slice={[0:1536], [0:4096]} | slice | bytes 25165824 | tf_op jit(solution)/shard_map/slice | solution.py:51
  248.7 21.2 %slice.18 = bf16[6,256,2,2048]{3,2,1,0:T(2,128)(2,1)} reshape(bf16[1536,4096]{1,0:T(8,128)(2,1)} %slice.26) | data formatting | bytes 25165824 | tf_op jit(solution)/shard_map/slice | solution.py:51
  269.8 30.7 %copy.30 = bf16[6,256,2,2048]{1,3,0,2:T(8,128)(2,1)} copy(bf16[6,256,2,2048]{3,2,1,0:T(2,128)(2,1)} %slice.18) | data formatting | bytes 25165824 | tf_op jit(solution)/shard_map/slice | solution.py:51
  300.6 8.3 %pad_maximum_fusion = (bf16[7,256,1,2048]{1,3,0,2:T(8,128)(2,1)S(1)}, bf16[7,256,1,2048]{1,3,0,2:T(8,128)(2,1)}) fusion(bf16[6,256,2,2048]{1,3,0,2:T(8,128)(2,1)} %copy.30, bf16[1,256,2,2048]{1,3,0,2:T(8,128)(2,1)} %bitcast.13), kind=kLoop, calls=%fused_computation.7 | loop fusion | flops 7340032 | bytes 29360128 | tf_op jit(solution)/shard_map/concatenate | solution.py:51
  308.9 1.1 fusion.9
  310.0 3.0 copy-done.3
  313.0 2.8 fusion.22
  315.8 17.9 %convert_bitcast_fusion = bf16[7,64,16,128]{3,1,2,0:T(8,128)(2,1)} fusion(bf16[7,256,16,128]{1,3,2,0:T(8,128)(2,1)} %bitcast.63, f32[7,16,64]{2,1,0:T(8,128)S(1)} %fusion.22, f32[7,16,256,64]{2,3,1,0:T(8,128)} %copy-done.3), kind=kOutput, calls=%fused_computation.20 | convolution fusion | flops 479862016 | bytes 16543744 | tf_op jit(solution)/shard_map/chqk,ckhd->cqhd/dot_general | solution.py:62
  333.7 2.7 copy.34
  336.4 1.7 reshape.131
  (18 shorter events, 0.2 us)
Async XLA Ops:
  6.5 12.2 %copy-start = (bf16[4,128,896]{2,1,0:T(8,128)(2,1)S(1)}, bf16[4,128,896]{2,1,0:T(8,128)(2,1)}, u32[]{:S(2)}) copy-start(bf16[4,128,896]{2,1,0:T(8,128)(2,1)} %param.6) | copy-start | bytes 2752516
  30.0 7.7 %copy-start.4 = (s32[1,14]{1,0:T(1,128)S(1)}, s32[1,14]{1,0:T(1,128)}, u32[]{:S(2)}) copy-start(s32[1,14]{1,0:T(1,128)} %param.7) | copy-start | bytes 172
  30.0 167.1 %all-to-all-start.1 = ((bf16[16,2,128,896]{3,2,1,0:T(8,128)(2,1)}), bf16[16,2,128,896]{3,2,1,0:T(8,128)(2,1)}, u32[]{:S(2)}, u32[]{:S(2)}) async-start(bf16[16,2,128,896]{3,2,1,0:T(8,128)(2,1)} %broadcast_select_fusion), calls=%async_computation.1 | async-start | bytes 14680064 | tf_op jit(solution)/shard_map/all_to_all | solution.py:38
  37.0 95.5 %all-gather.2.cloned.1.call-start = ((), (), s32[]{:S(2)}) async-start(), calls=%async_computation.2 | async-start | bytes 11010048 | tf_op jit(solution)/shard_map/all_gather | solution.py:45
  223.1 5.2 %copy-start.2 = (bf16[1792,4096]{1,0:T(8,128)(2,1)}, bf16[1792,4096]{1,0:T(8,128)(2,1)S(1)}, u32[]{:S(2)}) copy-start(bf16[1792,4096]{1,0:T(8,128)(2,1)S(1)} %convolution_convert_fusion) | copy-start | bytes 44040196
  231.1 69.5 %collective-permute-start = (bf16[256,2,2048]{0,2,1:T(8,128)(2,1)}, bf16[256,2,2048]{0,2,1:T(8,128)(2,1)}, u32[]{:S(2)}, u32[]{:S(2)}) collective-permute-start(bf16[256,2,2048]{0,2,1:T(8,128)(2,1)} %bitcast.67), channel_id=1, source_target_pairs={{0,1},{2,3},{4,5},{6,7},{8,9},{10,11},{12,13},{14,15},{16,17},{18,... | collective-permute-start | bytes 6291464 | tf_op jit(solution)/shard_map/ppermute | solution.py:13
  310.0 3.0 copy-start.3
  315.8 22.4 %copy-start.1 = (bf16[4,128,896]{2,1,0:T(8,128)(2,1)S(1)}, bf16[4,128,896]{2,1,0:T(8,128)(2,1)}, u32[]{:S(2)}) copy-start(bf16[4,128,896]{2,1,0:T(8,128)(2,1)} %param.6) | copy-start | bytes 2752516
Sparse Core Ops, SparseCore 0:
  39.4 93.1 all-gather.1
where the time goes:
time: 347 us; the launch traced here: 345 us
  waiting for transfers between devices  149 us (43%)
  local copies, waits for them, and re-layouts  101 us (29%)
  matrix products  36.9 us (11%)
  other arithmetic  22.1 us (6%)
  between operations  13.5 us (4%)
  starting transfers between devices  11.7 us (3%)
  blocking collectives  10.1 us (3%)
    all_gather x1, waiting for transfers between devices, per_device(): full_weight = lax.all_gather(kv_weight, 'seq', axis=0, tiled=True)  94.7 us
    slice x3, local copies, waits for them, and re-layouts, per_device(): keyvals = jnp.concatenate([earlier[None], blocks[:-1]], axis=0)  62.8 us
    all_to_all x1, waiting for transfers between devices, per_device(): lax.all_to_all(picked, 'db', split_axis=0, concat_axis=0, tiled=True)  53.8 us
    unnamed x12, local copies, waits for them, and re-layouts  20.9 us
    dot_general x1, matrix products, per_device(): jnp.einsum('chqk,ckhd->cqhd', probs, values, preferred_element_type=jnp.f...  17.9 us
    dot_general x1, matrix products, per_device(): jnp.dot(rows, full_weight.reshape(full_weight.shape[0], -1), preferred_el...  17.8 us
    all_to_all x1, blocking collectives, per_device(): lax.all_to_all(request.reshape(n_db, cap), 'db', split_axis=0, concat_axi...  10.1 us
    concatenate x1, other arithmetic, per_device(): keyvals = jnp.concatenate([earlier[None], blocks[:-1]], axis=0)  8.33 us
  transfers between devices with their start and end apart: 3, of which 2 were waited for; matrix products, arithmetic and copies ran while one was open for 22% of the time, Pallas kernels for 0%

commit v1 on v0

v1 whole, which is shorter than its diff:
```python
import functools

import jax
import jax.numpy as jnp
from jax import lax
from jax.experimental import pallas as pl
from jax.experimental.pallas import tpu as pltpu
from jax.sharding import PartitionSpec as P

HD = 128
KNN = 2
MESH = pl.DeviceIdType.MESH


def attend(nz, ny, nc, nx, parts, *refs):
    q_hbm, db_hbm, ids_ref, w_hbm, out_ref = refs[:5]
    gathered = refs[5:5 + parts]
    (w_all, kv, q_all, rows, ids_in, ids_own_s, ids_in_s, z_send, z_recv, y_send, y_recv,
     c_send, c_recv, x_send, x_recv, wc_send, wc_recv, i_send, i_recv, local) = refs[5 + parts:]
    d = lax.axis_index("db")
    x = lax.axis_index("seq")
    core = lax.rem(d, nc)
    y = lax.rem(d // nc, ny)
    z = d // (nc * ny)
    held, tokens, enc = db_hbm.shape
    step = tokens // parts
    w_rows = w_hbm.shape[0]
    share = w_rows // nc
    slots = kv.shape[0]
    span = KNN * tokens
    cols = w_all.shape[1]
    width = cols // 2
    stretches = slots // KNN
    length = q_all.shape[0] // stretches

    def index(zz, yy, cc):
        return (zz * ny + yy) * nc + cc

    others_z = [lax.rem(z + r, nz) for r in range(1, nz)]
    other_y = lax.rem(y + 1, ny)
    sibling = index(z, y, lax.rem(core + 1, nc))
    others_x = [lax.rem(x + r, nx) for r in range(1, nx)]
    across_y = index(z, other_y, core)

    barrier = pltpu.get_barrier_semaphore()
    peers = [{"db": index(zz, y, core)} for zz in others_z]
    peers += [{"seq": xx} for xx in others_x]
    if ny > 1:
        peers.append({"db": across_y})
    if nc > 1:
        peers.append({"db": sibling})
    for peer in peers:
        pl.semaphore_signal(barrier, inc=1, device_id=peer, device_id_type=MESH)
    pl.semaphore_wait(barrier, len(peers))

    def cell(k, zz, yy, cc):
        return gathered[k].at[pl.ds(held * index(zz, yy, cc), held)]

    def mine(k):
        return db_hbm.at[:, pl.ds(k * step, step), :]

    def along_z(k, to, source):
        return pltpu.make_async_remote_copy(
            src_ref=mine(k), dst_ref=cell(k, source, y, core), send_sem=z_send.at[k, to],
            recv_sem=z_recv.at[k, source], device_id={"db": index(to, y, core)}, device_id_type=MESH)

    def along_y(k, zz, yy, own):
        return pltpu.make_async_remote_copy(
            src_ref=mine(k) if own else cell(k, zz, yy, core), dst_ref=cell(k, zz, yy, core),
            send_sem=y_send.at[k, zz], recv_sem=y_recv.at[k, zz],
            device_id={"db": across_y}, device_id_type=MESH)

    def to_core(k, zz, yy, cc, own):
        return pltpu.make_async_remote_copy(
            src_ref=mine(k) if own else cell(k, zz, yy, cc), dst_ref=cell(k, zz, yy, cc),
            send_sem=c_send.at[k, zz, yy], recv_sem=c_recv.at[k, zz, yy],
            device_id={"db": sibling}, device_id_type=MESH)

    def weight_rows(xx, cc):
        return w_all.at[pl.ds(pl.multiple_of(xx * w_rows + cc * share, 16), share)]

    def along_x(to, source):
        return pltpu.make_async_remote_copy(
            src_ref=w_hbm.at[pl.ds(pl.multiple_of(core * share, 16), share)], dst_ref=weight_rows(source, core),
            send_sem=x_send.at[to], recv_sem=x_recv.at[source],
            device_id={"seq": to}, device_id_type=MESH)

    def weight_to_core(xx, cc):
        return pltpu.make_async_remote_copy(
            src_ref=weight_rows(xx, cc), dst_ref=weight_rows(xx, cc),
            send_sem=wc_send.at[xx], recv_sem=wc_recv.at[xx],
            device_id={"db": sibling}, device_id_type=MESH)

    def send_own(k):
        for zz in others_z:
            along_z(k, zz, z).start()
        if ny > 1:
            along_y(k, z, y, True).start()
        if nc > 1:
            to_core(k, z, y, core, True).start()

    def pass_z(k):
        for zz in others_z:
            along_z(k, z, zz).wait_recv()
            if ny > 1:
                along_y(k, zz, y, False).start()
            if nc > 1:
                to_core(k, zz, y, core, False).start()

    def pass_y(k):
        if ny > 1:
            for zz in [z] + others_z:
                along_y(k, zz, other_y, False).wait_recv()
                if nc > 1:
                    to_core(k, zz, other_y, core, False).start()
        if nc > 1:
            cc = lax.rem(core + 1, nc)
            for yy in range(ny):
                for zz in range(nz):
                    to_core(k, zz, yy, cc, False).wait_recv()

    ids = pltpu.make_async_remote_copy(
        src_ref=ids_ref, dst_ref=ids_in, send_sem=i_send, recv_sem=i_recv,
        device_id={"seq": lax.rem(x + 1, nx)}, device_id_type=MESH)
    ids.start()
    for k in range(min(2, parts)):
        send_own(k)
        if k == 0:
            for xx in others_x:
                along_x(xx, x).start()
    stay = [pltpu.make_async_copy(mine(k), cell(k, z, y, core), local.at[k]) for k in range(parts)]
    stay.append(pltpu.make_async_copy(
        w_hbm, w_all.at[pl.ds(pl.multiple_of(x * w_rows, 16), w_rows)], local.at[parts]))
    stay.append(pltpu.make_async_copy(q_hbm.at[0], q_all, local.at[parts + 1]))
    stay.append(pltpu.make_async_copy(ids_ref, ids_own_s, local.at[parts + 2]))
    for copy in stay:
        copy.start()
    ids.wait()
    inward = pltpu.make_async_copy(ids_in, ids_in_s, local.at[parts + 3])
    inward.start()
    inward.wait()
    for copy in stay:
        copy.wait()

    def project(k):
        for j in range(slots):
            if j < KNN:
                block = gathered[k][ids_in_s[0, slots - KNN + j]]
                block = jnp.where(x > 0, block, jnp.zeros_like(block))
            else:
                block = gathered[k][ids_own_s[0, j - KNN]]
            rows[j * step:(j + 1) * step, :] = block
        tile = 512

        @pl.loop(0, cols // tile)
        def _(t):
            at = pl.ds(pl.multiple_of(t * tile, tile), tile)
            got = jnp.dot(rows[...], w_all[:, at], preferred_element_type=jnp.float32)
            kv[:, k * step:(k + 1) * step, at] = got.astype(jnp.bfloat16).reshape(slots, step, tile)

    for k in range(parts):
        if k + 2 < parts:
            send_own(k + 2)
        pass_z(k)
        if k == 1 or parts == 1:
            for xx in others_x:
                along_x(x, xx).wait_recv()
                if nc > 1:
                    weight_to_core(xx, core).start()
            if nc > 1:
                for xx in others_x:
                    weight_to_core(xx, lax.rem(core + 1, nc)).wait_recv()
        if k > 0:
            pass_y(k - 1)
            project(k - 1)
    pass_y(parts - 1)
    project(parts - 1)

    @pl.loop(0, stretches)
    def _(c):
        tok = pl.ds(pl.multiple_of(c * length, length), length)
        for h in range(width // HD):
            query = q_all[tok, h * HD:(h + 1) * HD]
            keys = kv[pl.ds(c * KNN, KNN), :, h * HD:(h + 1) * HD].reshape(span, HD)
            values = kv[pl.ds(c * KNN, KNN), :, width + h * HD:width + (h + 1) * HD].reshape(span, HD)
            scores = lax.dot_general(query, keys, (((1,), (1,)), ((), ())), preferred_element_type=jnp.float32)
            scores = scores * HD ** (-0.5)
            top = jnp.max(scores, axis=-1, keepdims=True)
            weights = jnp.exp(scores - top)
            probs = (weights / jnp.sum(weights, axis=-1, keepdims=True)).astype(jnp.bfloat16)
            mixed = jnp.dot(probs, values, preferred_element_type=jnp.float32)
            out_ref[0, tok, h * HD:(h + 1) * HD] = mixed.astype(jnp.bfloat16)

    for k in range(parts):
        for zz in others_z:
            along_z(k, zz, z).wait_send()
        if ny > 1:
            along_y(k, z, y, True).wait_send()
            for zz in others_z:
                along_y(k, zz, y, False).wait_send()
        if nc > 1:
            to_core(k, z, y, core, True).wait_send()
            for zz in others_z:
                to_core(k, zz, y, core, False).wait_send()
            for zz in [z] + others_z:
                if ny > 1:
                    to_core(k, zz, other_y, core, False).wait_send()
    for xx in others_x:
        along_x(xx, x).wait_send()
        if nc > 1:
            weight_to_core(xx, core).wait_send()


def solution(mesh):
    n_db, nx = mesh.shape["db"], mesh.shape["seq"]
    nc = 2 if mesh.shape["mp"] == 1 and n_db % 2 == 0 else 1
    ny = 2 if mesh.shape["groups"] == 1 and (n_db // nc) % 2 == 0 else 1
    nz = n_db // (nc * ny)
    parts = 4

    def per_device(queries, database, nb_owner, nb_row, kv_weight):
        held, tokens, enc = database.shape
        slots = nb_owner.shape[1]
        w_rows, _, head_cols = kv_weight.shape
        weight = kv_weight.reshape(w_rows, 2 * head_cols)
        ids = jnp.pad(nb_owner * held + nb_row, ((0, 7), (0, 128 - slots)))
        step = tokens // parts
        anywhere = pl.BlockSpec(memory_space=pl.ANY)
        vmem = pl.BlockSpec(memory_space=pltpu.VMEM)
        sem = pltpu.SemaphoreType.DMA
        flops = 2 * slots * tokens * enc * 2 * head_cols
        return pl.pallas_call(
            functools.partial(attend, nz, ny, nc, nx, parts),
            out_shape=jax.ShapeDtypeStruct(queries.shape, jnp.bfloat16),
            in_specs=[anywhere, anywhere, vmem, anywhere],
            out_specs=vmem,
            scratch_shapes=[pltpu.VMEM((n_db * held, step, enc), jnp.bfloat16) for _ in range(parts)] + [
                pltpu.VMEM((nx * w_rows, 2 * head_cols), jnp.bfloat16),
                pltpu.VMEM((slots, tokens, 2 * head_cols), jnp.bfloat16),
                pltpu.VMEM(queries.shape[1:], jnp.bfloat16),
                pltpu.VMEM((slots * step, enc), jnp.bfloat16),
                pltpu.VMEM((8, 128), jnp.int32),
                pltpu.SMEM((8, 128), jnp.int32),
                pltpu.SMEM((8, 128), jnp.int32),
                sem((parts, nz)), sem((parts, nz)),
                sem((parts, nz)), sem((parts, nz)),
                sem((parts, nz, ny)), sem((parts, nz, ny)),
                sem((nx,)), sem((nx,)),
                sem((nx,)), sem((nx,)),
                sem, sem,
                sem((parts + 4,)),
            ],
            compiler_params=pltpu.CompilerParams(
                collective_id=0, has_side_effects=True, vmem_limit_bytes=60 * 2 ** 20),
            cost_estimate=pl.CostEstimate(flops=flops, bytes_accessed=20 * 2 ** 20, transcendentals=0),
        )(queries, database, ids, weight)

    return jax.shard_map(
        per_device,
        mesh=mesh,
        in_specs=(
            P(("groups", "db"), "seq", "mp"),
            P(("groups", "db"), None, None),
            P(("groups", "db"), "seq"),
            P(("groups", "db"), "seq"),
            P("seq", None, "mp"),
        ),
        out_specs=P(("groups", "db"), "seq", "mp"),
        check_vma=False,
    )
```

time: 347 us -> 166 us (0.48)
  the two profiles are of different devices: /device:TPU:16 before, /device:TPU:11 now
where the time goes in v1:
time: 166 us
  Pallas kernels  156 us (94%)
  local copies, waits for them, and re-layouts  9.44 us (6%)
    pallas_call x1, Pallas kernels, per_device(): pl.pallas_call(functools.partial(attend, nz, ny, nc, nx, parts), out_shap...  156 us
    unnamed x2, local copies, waits for them, and re-layouts  8.84 us

profile of v1, /device:TPU:11, one launch (start us, length us, event | category | flops | bytes accessed | tf_op | source)
XLA Modules:
  0.0 166.3 jit_solution(9627261065450955793)
XLA Ops:
  0.0 0.7 multiply_add_fusion
  0.7 0.6 pad.4.refs_2_
  1.3 5.9 %copy.6 = bf16[56,8,2,2048]{3,1,2,0:T(8,128)(2,1)} copy(bf16[56,8,2,2048]{3,2,1,0:T(2,128)(2,1)} %bitcast.2) | data formatting | bytes 7340032
  7.2 156.1 %shard_map.55 = bf16[1,448,2048]{2,1,0:T(8,128)(2,1)} custom-call(bf16[1,448,2048]{2,1,0:T(8,128)(2,1)} %refs_0_.1, bf16[4,128,896]{2,1,0:T(8,128)(2,1)} %refs_1_.1, s32[8,128]{1,0:T(8,128)} %pad.4.refs_2_, bf16[448,4096]{1,0:T(8,128)(2,1)} %bitcast.3), custom_call_target="tpu_custom_call" | custom-call | flops 13153337344 | bytes 20971520 | tf_op jit(solution)/shard_map/pallas_call | solution.py:232
  163.3 2.9 %copy.8 = bf16[1,448,2048]{2,1,0:T(8,128)(2,1)} copy(bf16[1,448,2048]{2,1,0:T(8,128)(2,1)} %shard_map.55) | data formatting | bytes 3670016

commit v2 on v1

v2 whole, which is shorter than its diff:
```python
import functools

import jax
import jax.numpy as jnp
from jax import lax
from jax.experimental import pallas as pl
from jax.experimental.pallas import tpu as pltpu
from jax.sharding import PartitionSpec as P

HD = 128
KNN = 2
MESH = pl.DeviceIdType.MESH


def attend(nz, ny, nc, nx, parts, *refs):
    q_hbm, db_hbm, ids_ref, w_hbm, out_ref = refs[:5]
    gathered = refs[5:5 + parts]
    (w_all, kv, q_all, rows, ids_in, ids_own_s, ids_in_s, up_send, down_send, z_recv, y_send, y_recv,
     c_send, c_recv, a_send, a_recv, x_send, x_recv, wc_send, wc_recv, i_send, i_recv, local) = refs[5 + parts:]
    d = lax.axis_index("db")
    x = lax.axis_index("seq")
    core = lax.rem(d, nc)
    y = lax.rem(d // nc, ny)
    z = d // (nc * ny)
    held, tokens, enc = db_hbm.shape
    step = tokens // parts
    w_rows = w_hbm.shape[0]
    share = w_rows // nc
    slots = kv.shape[0]
    span = KNN * tokens
    cols = w_all.shape[1]
    width = cols // 2
    stretches = slots // KNN
    length = q_all.shape[0] // stretches
    other_y = lax.rem(y + 1, ny)
    other_core = lax.rem(core + 1, nc)
    skips = {0: (1, 3), 1: (2, 4)} if ny > 1 and nx == 2 and parts > 4 else {}
    skipper = {k: xx for xx, ks in skips.items() for k in ks}

    def index(zz, yy, cc):
        return (zz * ny + yy) * nc + cc

    others_x = [lax.rem(x + r, nx) for r in range(1, nx)]
    up, down = index(z + 1, y, core), index(z - 1, y, core)
    sibling = {"db": index(z, y, other_core)}
    across_y = {"db": index(z, other_y, core)}

    barrier = pltpu.get_barrier_semaphore()
    peers = [{"seq": xx} for xx in others_x]
    if ny > 1:
        peers.append(across_y)
    if nc > 1:
        peers.append(sibling)
    for peer in peers:
        pl.semaphore_signal(barrier, inc=1, device_id=peer, device_id_type=MESH)

    @pl.when(z < nz - 1)
    def _():
        pl.semaphore_signal(barrier, inc=1, device_id={"db": up}, device_id_type=MESH)

    @pl.when(z > 0)
    def _():
        pl.semaphore_signal(barrier, inc=1, device_id={"db": down}, device_id_type=MESH)

    ends = jnp.where((z == 0) | (z == nz - 1), 1, 0)
    pl.semaphore_wait(barrier, len(peers) + 2 - ends)

    def cell(k, zz, yy, cc):
        return gathered[k].at[pl.ds(held * ((cc * ny + yy) * nz + zz), held)]

    def column(k, yy, cc):
        return gathered[k].at[pl.ds(held * nz * (cc * ny + yy), held * nz)]

    def mine(k):
        return db_hbm.at[:, pl.ds(k * step, step), :]

    def remote(src, dst, send, recv, to):
        return pltpu.make_async_remote_copy(
            src_ref=src, dst_ref=dst, send_sem=send, recv_sem=recv, device_id=to, device_id_type=MESH)

    def chain(k, zz, own, upward):
        return remote(mine(k) if own else cell(k, zz, y, core), cell(k, zz, y, core),
                      (up_send if upward else down_send).at[k, zz], z_recv.at[k, zz],
                      {"db": up if upward else down})

    def along_y(k, zz, yy, own):
        return remote(mine(k) if own else cell(k, zz, yy, core), cell(k, zz, yy, core),
                      y_send.at[k, zz], y_recv.at[k, zz], across_y)

    def to_core(k, yy, cc):
        return remote(column(k, yy, cc), column(k, yy, cc), c_send.at[k, yy], c_recv.at[k, yy], sibling)

    def around(k):
        return remote(column(k, other_y, core), column(k, other_y, core), a_send.at[k], a_recv.at[k],
                      {"seq": others_x[0]})

    def weight_rows(xx, cc):
        return w_all.at[pl.ds(pl.multiple_of(xx * w_rows + cc * share, 16), share)]

    def along_x(to, source):
        return remote(w_hbm.at[pl.ds(pl.multiple_of(core * share, 16), share)], weight_rows(source, core),
                      x_send.at[to], x_recv.at[source], {"seq": to})

    def weight_to_core(xx, cc):
        return remote(weight_rows(xx, cc), weight_rows(xx, cc), wc_send.at[xx], wc_recv.at[xx], sibling)

    def through_y(k, do):
        if ny > 1:
            if k in skipper:
                pl.when(x != skipper[k])(do)
            else:
                do()

    def send_own(k):
        pl.when(z < nz - 1)(lambda: chain(k, z, True, True).start())
        pl.when(z > 0)(lambda: chain(k, z, True, False).start())
        through_y(k, lambda: along_y(k, z, y, True).start())

    def pass_z(k):
        @pl.loop(1, nz)
        def _(t):
            @pl.when(z - t >= 0)
            def _():
                chain(k, z - t, False, True).wait_recv()
                pl.when(z < nz - 1)(lambda: chain(k, z - t, False, True).start())
                through_y(k, lambda: along_y(k, z - t, y, False).start())

            @pl.when(z + t < nz)
            def _():
                chain(k, z + t, False, False).wait_recv()
                pl.when(z > 0)(lambda: chain(k, z + t, False, False).start())
                through_y(k, lambda: along_y(k, z + t, y, False).start())
        if nc > 1:
            stay[k].wait()
            to_core(k, y, core).start()

    def pass_y(k):
        def arrive():
            @pl.loop(0, nz)
            def _(zz):
                along_y(k, zz, other_y, False).wait_recv()
            if nc > 1:
                to_core(k, other_y, core).start()
            if k in skipper:
                around(k).start()
        through_y(k, arrive)

    def pass_x(k):
        if k in skipper:
            @pl.when(x == skipper[k])
            def _():
                around(k).wait_recv()
                if nc > 1:
                    to_core(k, other_y, core).start()

    def pass_core(k):
        if nc > 1:
            for yy in range(ny):
                to_core(k, yy, other_core).wait_recv()
        else:
            stay[k].wait()

    ids = remote(ids_ref, ids_in, i_send, i_recv, {"seq": lax.rem(x + 1, nx)})
    stay = [pltpu.make_async_copy(mine(k), cell(k, z, y, core), local.at[k]) for k in range(parts)]
    rest = [
        pltpu.make_async_copy(
            w_hbm, w_all.at[pl.ds(pl.multiple_of(x * w_rows, 16), w_rows)], local.at[parts]),
        pltpu.make_async_copy(q_hbm.at[0], q_all, local.at[parts + 1]),
        pltpu.make_async_copy(ids_ref, ids_own_s, local.at[parts + 2]),
    ]
    ids.start()
    ahead = 3
    for k in range(min(ahead, parts)):
        send_own(k)
        if k == 0:
            for xx in others_x:
                along_x(xx, x).start()
    for copy in stay + rest:
        copy.start()
    ids.wait()
    inward = pltpu.make_async_copy(ids_in, ids_in_s, local.at[parts + 3])
    inward.start()
    inward.wait()
    for copy in rest:
        copy.wait()

    def project(k):
        for j in range(slots):
            if j < KNN:
                block = gathered[k][ids_in_s[0, slots - KNN + j]]
                block = jnp.where(x > 0, block, jnp.zeros_like(block))
            else:
                block = gathered[k][ids_own_s[0, j - KNN]]
            rows[j * step:(j + 1) * step, :] = block
        tile = 512

        @pl.loop(0, cols // tile)
        def _(t):
            at = pl.ds(pl.multiple_of(t * tile, tile), tile)
            got = jnp.dot(rows[...], w_all[:, at], preferred_element_type=jnp.float32)
            kv[:, k * step:(k + 1) * step, at] = got.astype(jnp.bfloat16).reshape(slots, step, tile)

    late = min(4, parts - 1)
    done = 0
    for k in range(parts):
        if k + ahead < parts:
            send_own(k + ahead)
        pass_z(k)
        if k > 0:
            pass_y(k - 1)
        if k == late:
            for xx in others_x:
                along_x(x, xx).wait_recv()
                if nc > 1:
                    weight_to_core(xx, core).start()
            if nc > 1:
                for xx in others_x:
                    weight_to_core(xx, other_core).wait_recv()
        if k >= late:
            for _ in range(1 if k == late else 2):
                if done < k - 1:
                    pass_x(done)
                    pass_core(done)
                    project(done)
                    done += 1
    pass_y(parts - 1)
    for k in range(done, parts):
        pass_x(k)
        pass_core(k)
        project(k)

    @pl.loop(0, stretches)
    def _(c):
        tok = pl.ds(pl.multiple_of(c * length, length), length)
        heads, group = width // HD, 8
        sets = [range(at, min(at + group, heads)) for at in range(0, heads, group)]
        scores, probs = {}, {}
        for turn in range(len(sets) + 2):
            if turn < len(sets):
                for h in sets[turn]:
                    query = q_all[tok, h * HD:(h + 1) * HD]
                    keys = kv[pl.ds(c * KNN, KNN), :, h * HD:(h + 1) * HD].reshape(span, HD)
                    scores[h] = lax.dot_general(
                        query, keys, (((1,), (1,)), ((), ())), preferred_element_type=jnp.float32)
            if 1 <= turn <= len(sets):
                now = sets[turn - 1]
                top = {h: jnp.max(scores[h], axis=-1, keepdims=True) for h in now}
                weights = {h: jnp.exp((scores[h] - top[h]) * HD ** (-0.5)) for h in now}
                total = {h: jnp.sum(weights[h], axis=-1, keepdims=True) for h in now}
                for h in now:
                    probs[h] = (weights[h] * (1.0 / total[h])).astype(jnp.bfloat16)
            if turn >= 2:
                for h in sets[turn - 2]:
                    values = kv[pl.ds(c * KNN, KNN), :, width + h * HD:width + (h + 1) * HD].reshape(span, HD)
                    mixed = jnp.dot(probs[h], values, preferred_element_type=jnp.float32)
                    out_ref[0, tok, h * HD:(h + 1) * HD] = mixed.astype(jnp.bfloat16)
    for k in range(parts):
        @pl.loop(0, nz)
        def _(zz):
            pl.when((z < nz - 1) & (zz <= z))(lambda: chain(k, zz, False, True).wait_send())
            pl.when((z > 0) & (zz >= z))(lambda: chain(k, zz, False, False).wait_send())
            through_y(k, lambda: along_y(k, zz, y, False).wait_send())
        if nc > 1:
            for yy in range(ny):
                to_core(k, yy, core).wait_send()
        if k in skipper:
            pl.when(x != skipper[k])(lambda: around(k).wait_send())
    for xx in others_x:
        along_x(xx, x).wait_send()
        if nc > 1:
            weight_to_core(xx, core).wait_send()


def solution(mesh):
    n_db, nx = mesh.shape["db"], mesh.shape["seq"]
    nc = 2 if mesh.shape["mp"] == 1 and n_db % 2 == 0 else 1
    ny = 2 if mesh.shape["groups"] == 1 and (n_db // nc) % 2 == 0 else 1
    nz = n_db // (nc * ny)
    parts = 8

    def per_device(queries, database, nb_owner, nb_row, kv_weight):
        held, tokens, enc = database.shape
        slots = nb_owner.shape[1]
        w_rows, _, head_cols = kv_weight.shape
        weight = kv_weight.reshape(w_rows, 2 * head_cols)
        zy, core = nb_owner // nc, nb_owner % nc
        place = (core * ny + zy % ny) * nz + zy // ny
        ids = jnp.pad(place * held + nb_row, ((0, 7), (0, 128 - slots)))
        step = tokens // parts
        anywhere = pl.BlockSpec(memory_space=pl.ANY)
        vmem = pl.BlockSpec(memory_space=pltpu.VMEM)
        sem = pltpu.SemaphoreType.DMA
        flops = 2 * slots * tokens * enc * 2 * head_cols
        return pl.pallas_call(
            functools.partial(attend, nz, ny, nc, nx, parts),
            out_shape=jax.ShapeDtypeStruct(queries.shape, jnp.bfloat16),
            in_specs=[anywhere, anywhere, vmem, anywhere],
            out_specs=vmem,
            scratch_shapes=[pltpu.VMEM((n_db * held, step, enc), jnp.bfloat16) for _ in range(parts)] + [
                pltpu.VMEM((nx * w_rows, 2 * head_cols), jnp.bfloat16),
                pltpu.VMEM((slots, tokens, 2 * head_cols), jnp.bfloat16),
                pltpu.VMEM(queries.shape[1:], jnp.bfloat16),
                pltpu.VMEM((slots * step, enc), jnp.bfloat16),
                pltpu.VMEM((8, 128), jnp.int32),
                pltpu.SMEM((8, 128), jnp.int32),
                pltpu.SMEM((8, 128), jnp.int32),
                sem((parts, nz)), sem((parts, nz)), sem((parts, nz)),
                sem((parts, nz)), sem((parts, nz)),
                sem((parts, ny)), sem((parts, ny)),
                sem((parts,)), sem((parts,)),
                sem((nx,)), sem((nx,)),
                sem((nx,)), sem((nx,)),
                sem, sem,
                sem((parts + 4,)),
            ],
            compiler_params=pltpu.CompilerParams(
                collective_id=0, has_side_effects=True, vmem_limit_bytes=60 * 2 ** 20),
            cost_estimate=pl.CostEstimate(flops=flops, bytes_accessed=20 * 2 ** 20, transcendentals=0),
        )(queries, database, ids, weight)

    return jax.shard_map(
        per_device,
        mesh=mesh,
        in_specs=(
            P(("groups", "db"), "seq", "mp"),
            P(("groups", "db"), None, None),
            P(("groups", "db"), "seq"),
            P(("groups", "db"), "seq"),
            P("seq", None, "mp"),
        ),
        out_specs=P(("groups", "db"), "seq", "mp"),
        check_vma=False,
    )
```

time: 166 us -> 118 us (0.71)
  the two profiles are of different devices: /device:TPU:11 before, /device:TPU:0 now
where the time goes in v2:
time: 118 us
  Pallas kernels  108 us (92%)
  local copies, waits for them, and re-layouts  9.44 us (8%)
    pallas_call x1, Pallas kernels, per_device(): pl.pallas_call(functools.partial(attend, nz, ny, nc, nx, parts), out_shap...  108 us
    unnamed x2, local copies, waits for them, and re-layouts  8.84 us

profile of v2, /device:TPU:0, one launch (start us, length us, event | category | flops | bytes accessed | tf_op | source)
XLA Modules:
  0.0 118.0 jit_solution(1850324335822981987)
XLA Ops:
  0.0 0.7 multiply_add_fusion
  0.7 0.6 pad.4.refs_2_
  1.3 5.9 %copy.6 = bf16[56,8,2,2048]{3,1,2,0:T(8,128)(2,1)} copy(bf16[56,8,2,2048]{3,2,1,0:T(2,128)(2,1)} %bitcast.2) | data formatting | bytes 7340032
  7.2 107.9 %shard_map.55 = bf16[1,448,2048]{2,1,0:T(8,128)(2,1)} custom-call(bf16[1,448,2048]{2,1,0:T(8,128)(2,1)} %refs_0_.1, bf16[4,128,896]{2,1,0:T(8,128)(2,1)} %refs_1_.1, s32[8,128]{1,0:T(8,128)} %pad.4.refs_2_, bf16[448,4096]{1,0:T(8,128)(2,1)} %bitcast.3), custom_call_target="tpu_custom_call" | custom-call | flops 13153337344 | bytes 20971520 | tf_op jit(solution)/shard_map/pallas_call | solution.py:294
  115.1 2.9 %copy.8 = bf16[1,448,2048]{2,1,0:T(8,128)(2,1)} copy(bf16[1,448,2048]{2,1,0:T(8,128)(2,1)} %shard_map.55) | data formatting | bytes 3670016

commit v3 on v2

--- a/solution.py
+++ b/solution.py
@@ -62,7 +62,7 @@
     def _():
         pl.semaphore_signal(barrier, inc=1, device_id={"db": down}, device_id_type=MESH)
 
-    ends = jnp.where((z == 0) | (z == nz - 1), 1, 0)
+    ends = jnp.where(z == 0, 1, 0) + jnp.where(z == nz - 1, 1, 0)
     pl.semaphore_wait(barrier, len(peers) + 2 - ends)
 
     def cell(k, zz, yy, cc):
@@ -116,9 +116,8 @@
         pl.when(z > 0)(lambda: chain(k, z, True, False).start())
         through_y(k, lambda: along_y(k, z, y, True).start())
 
-    def pass_z(k):
-        @pl.loop(1, nz)
-        def _(t):
+    def pass_z(k, beside):
+        def hop(t):
             @pl.when(z - t >= 0)
             def _():
                 chain(k, z - t, False, True).wait_recv()
@@ -130,6 +129,17 @@
                 chain(k, z + t, False, False).wait_recv()
                 pl.when(z > 0)(lambda: chain(k, z + t, False, False).start())
                 through_y(k, lambda: along_y(k, z + t, y, False).start())
+
+        hops = nz - 1
+        if beside and hops < 8:
+            for t in range(1, nz):
+                hop(t)
+                for work in beside[(t - 1) * len(beside) // hops:t * len(beside) // hops]:
+                    work()
+        else:
+            pl.loop(1, nz)(hop)
+            for work in beside:
+                work()
         if nc > 1:
             stay[k].wait()
             to_core(k, y, core).start()
@@ -184,7 +194,7 @@
     for copy in rest:
         copy.wait()
 
-    def project(k):
+    def pick(k):
         for j in range(slots):
             if j < KNN:
                 block = gathered[k][ids_in_s[0, slots - KNN + j]]
@@ -192,20 +202,36 @@
             else:
                 block = gathered[k][ids_own_s[0, j - KNN]]
             rows[j * step:(j + 1) * step, :] = block
-        tile = 512
-
-        @pl.loop(0, cols // tile)
+
+    tile = 512
+    tiles = cols // tile
+
+    def project(k, first, last):
+        @pl.loop(first, last)
         def _(t):
             at = pl.ds(pl.multiple_of(t * tile, tile), tile)
             got = jnp.dot(rows[...], w_all[:, at], preferred_element_type=jnp.float32)
             kv[:, k * step:(k + 1) * step, at] = got.astype(jnp.bfloat16).reshape(slots, step, tile)
+
+    def steps_of(k):
+        def begin():
+            pass_x(k)
+            pass_core(k)
+            pick(k)
+        return [begin] + [functools.partial(project, k, t, t + 2) for t in range(0, tiles, 2)]
 
     late = min(4, parts - 1)
     done = 0
     for k in range(parts):
         if k + ahead < parts:
             send_own(k + ahead)
-        pass_z(k)
+        beside = []
+        if k > late:
+            for _ in range(2):
+                if done < k - 1:
+                    beside += steps_of(done)
+                    done += 1
+        pass_z(k, beside)
         if k > 0:
             pass_y(k - 1)
         if k == late:
@@ -216,18 +242,11 @@
             if nc > 1:
                 for xx in others_x:
                     weight_to_core(xx, other_core).wait_recv()
-        if k >= late:
-            for _ in range(1 if k == late else 2):
-                if done < k - 1:
-                    pass_x(done)
-                    pass_core(done)
-                    project(done)
-                    done += 1
-    pass_y(parts - 1)
     for k in range(done, parts):
-        pass_x(k)
-        pass_core(k)
-        project(k)
+        if k == parts - 1:
+            pass_y(k)
+        for work in steps_of(k):
+            work()
 
     @pl.loop(0, stretches)
     def _(c):

time: 118 us -> 115 us (0.975)
  Pallas kernels: 108 us -> 104 us
    pallas_call x1, Pallas kernels: 108 us -> 104 us  [per_device(): pl.pallas_call(functools.partial(attend, nz, ny, nc, nx, parts), out_shap...]
where the time goes in v3:
time: 115 us; the launch traced here: 114 us
  Pallas kernels  104 us (90%)
  local copies, waits for them, and re-layouts  9.44 us (8%)
    pallas_call x1, Pallas kernels, per_device(): pl.pallas_call(functools.partial(attend, nz, ny, nc, nx, parts), out_shap...  104 us
    unnamed x2, local copies, waits for them, and re-layouts  8.84 us

profile of v3, /device:TPU:0, one launch (start us, length us, event | category | flops | bytes accessed | tf_op | source)
XLA Modules:
  0.0 114.4 jit_solution(4597838969871114431)
XLA Ops:
  0.0 0.7 multiply_add_fusion
  0.7 0.6 pad.4.refs_2_
  1.3 5.9 %copy.6 = bf16[56,8,2,2048]{3,1,2,0:T(8,128)(2,1)} copy(bf16[56,8,2,2048]{3,2,1,0:T(2,128)(2,1)} %bitcast.2) | data formatting | bytes 7340032
  7.2 104.3 %shard_map.55 = bf16[1,448,2048]{2,1,0:T(8,128)(2,1)} custom-call(bf16[1,448,2048]{2,1,0:T(8,128)(2,1)} %refs_0_.1, bf16[4,128,896]{2,1,0:T(8,128)(2,1)} %refs_1_.1, s32[8,128]{1,0:T(8,128)} %pad.4.refs_2_, bf16[448,4096]{1,0:T(8,128)(2,1)} %bitcast.3), custom_call_target="tpu_custom_call" | custom-call | flops 13153337344 | bytes 20971520 | tf_op jit(solution)/shard_map/pallas_call | solution.py:313
  111.5 2.9 %copy.8 = bf16[1,448,2048]{2,1,0:T(8,128)(2,1)} copy(bf16[1,448,2048]{2,1,0:T(8,128)(2,1)} %shard_map.55) | data formatting | bytes 3670016

commit v4 on v3

--- a/solution.py
+++ b/solution.py
@@ -203,7 +203,7 @@
                 block = gathered[k][ids_own_s[0, j - KNN]]
             rows[j * step:(j + 1) * step, :] = block
 
-    tile = 512
+    tile = 1024
     tiles = cols // tile
 
     def project(k, first, last):
@@ -218,7 +218,7 @@
             pass_x(k)
             pass_core(k)
             pick(k)
-        return [begin] + [functools.partial(project, k, t, t + 2) for t in range(0, tiles, 2)]
+        return [begin] + [functools.partial(project, k, t, t + 1) for t in range(0, tiles, 1)]
 
     late = min(4, parts - 1)
     done = 0

time: 115 us -> 109 us (0.948)
  Pallas kernels: 104 us -> 98.5 us
    pallas_call x1, Pallas kernels: 104 us -> 98.5 us  [per_device(): pl.pallas_call(functools.partial(attend, nz, ny, nc, nx, parts), out_shap...]
where the time goes in v4:
time: 109 us
  Pallas kernels  98.5 us (90%)
  local copies, waits for them, and re-layouts  9.44 us (9%)
    pallas_call x1, Pallas kernels, per_device(): pl.pallas_call(functools.partial(attend, nz, ny, nc, nx, parts), out_shap...  98.5 us
    unnamed x2, local copies, waits for them, and re-layouts  8.84 us

profile of v4, /device:TPU:0, one launch (start us, length us, event | category | flops | bytes accessed | tf_op | source)
XLA Modules:
  0.0 108.6 jit_solution(18361675438905397350)
XLA Ops:
  0.0 0.7 multiply_add_fusion
  0.7 0.6 pad.4.refs_2_
  1.3 5.9 %copy.6 = bf16[56,8,2,2048]{3,1,2,0:T(8,128)(2,1)} copy(bf16[56,8,2,2048]{3,2,1,0:T(2,128)(2,1)} %bitcast.2) | data formatting | bytes 7340032
  7.2 98.5 %shard_map.55 = bf16[1,448,2048]{2,1,0:T(8,128)(2,1)} custom-call(bf16[1,448,2048]{2,1,0:T(8,128)(2,1)} %refs_0_.1, bf16[4,128,896]{2,1,0:T(8,128)(2,1)} %refs_1_.1, s32[8,128]{1,0:T(8,128)} %pad.4.refs_2_, bf16[448,4096]{1,0:T(8,128)(2,1)} %bitcast.3), custom_call_target="tpu_custom_call" | custom-call | flops 13153337344 | bytes 20971520 | tf_op jit(solution)/shard_map/pallas_call | solution.py:313
  105.7 2.9 %copy.8 = bf16[1,448,2048]{2,1,0:T(8,128)(2,1)} copy(bf16[1,448,2048]{2,1,0:T(8,128)(2,1)} %shard_map.55) | data formatting | bytes 3670016
